TPU v7x, 32 devices: a whole 2x2x4 slice. The times are simulated.
32 devices in a mesh: groups: 2 (over y), flat: 4 (over z), dp: 4 (over x, core).
Axes of the slice: x: 2, y: 2, z: 4, core: 2. Of those that a mesh axis runs over, the one named last changes fastest.
Arguments:
- activations: bfloat16 [4096, 14336], P(('groups', 'dp'), 'flat'), parts along dimension 0
- curvature: float32 [4096], P(('groups', 'dp')), parts along dimension 0, may hold values from 0.3 to 3
- vector_now: float32 [28672, 4096], P(('groups', 'flat', 'dp')), parts along dimension 0
- vector_before: float32 [28672, 4096], P(('groups', 'flat', 'dp')), parts along dimension 0, may hold values from -6 to 6
- sign_bits: int32 [28672, 4096], P(('groups', 'flat', 'dp')), parts along dimension 0, may hold values from 0 to 1
- prior_precision: float32 [2], P('groups'), parts along dimension 0, may hold values from 0.2 to 2
- beta_before: float32 [2], P('groups'), parts along dimension 0, may hold values from 0.3 to 1.5
- kept_rows: int32 [8192], P('groups'), parts along dimension 0, may hold values from 0 to 3583
- kept_cols: int32 [8192], P('groups'), parts along dimension 0, may hold values from 0 to 16383
Outputs:
- vector_next: float32 [28672, 4096], P(('groups', 'flat', 'dp')), parts along dimension 0
- alpha_value: float32 [2], P('groups'), parts along dimension 0
- beta_value: float32 [2], P('groups'), parts along dimension 0
- sketch: float32 [8192], P('groups'), parts along dimension 0
There are 2 independent parts, one for each index of `groups`. A program takes and returns all parts, laid end to end along the dimension named above; each array names one. Nothing has to cross between parts.
All inputs are finite; a program needn't handle non-finite values.
Results may differ from a plain program's by a relative error of at most 0.015.
Values may be sent and summed in bfloat16 or wider, within the bound.
A program may use at most 256 MiB of HBM per device.

v0:
```python
import math
import jax
import jax.numpy as jnp
from jax import lax
from jax.sharding import PartitionSpec as P

BLOCK = 128


def parity_sign(row_index, col_index):
    common_bits = jnp.bitwise_and(row_index, col_index)
    parity_sum = jnp.zeros_like(common_bits)
    for position in range(BLOCK.bit_length() - 1):
        parity_sum = parity_sum + jnp.bitwise_and(jnp.right_shift(common_bits, position), 1)
    return (1 - 2 * jnp.bitwise_and(parity_sum, 1)).astype(jnp.float32) / math.sqrt(BLOCK)


def hadamard_table():
    row_index = lax.broadcasted_iota(jnp.int32, (BLOCK, BLOCK), 0)
    col_index = lax.broadcasted_iota(jnp.int32, (BLOCK, BLOCK), 1)
    return parity_sign(row_index, col_index)


def pick_dense(column_block, hadamard, own_index, kept_rows, kept_cols):
    cols_here = column_block.shape[1]
    section_two = jnp.einsum(
        "ri,bic->brc",
        hadamard,
        column_block.reshape(-1, BLOCK, cols_here),
        precision=lax.Precision.HIGHEST,
    )
    section_two = section_two.reshape(-1, cols_here)
    first_col = own_index * cols_here
    inside = jnp.logical_and(kept_cols >= first_col, kept_cols < first_col + cols_here)
    local_col = jnp.clip(kept_cols - first_col, 0, cols_here - 1)
    return jnp.where(inside, section_two[kept_rows, local_col], 0.0)


def on_device(
    activations,
    curvature,
    vector_now,
    vector_before,
    sign_bits,
    prior_precision,
    beta_before,
    kept_rows,
    kept_cols,
):
    token_count = activations.shape[0]
    out_width = vector_now.shape[1]
    local_rows = vector_now.shape[0]
    flat_count = lax.axis_size("flat")
    data_count = lax.axis_size("dp")
    total_tokens = token_count * data_count
    total_cells = local_rows * out_width * flat_count * data_count
    vector_half = vector_now.astype(jnp.bfloat16)
    columns = activations
    partial_out = jnp.dot(
        columns,
        lax.all_gather(vector_half, "dp", axis=0, tiled=True),
        preferred_element_type=jnp.float32,
    )
    shares = lax.psum_scatter(
        partial_out.astype(jnp.bfloat16), "flat", scatter_dimension=1, tiled=True
    ).astype(jnp.float32)
    scaled_share = (curvature[:, None] * shares / total_tokens).astype(jnp.bfloat16)
    scaled = lax.all_gather(scaled_share, "flat", axis=1, tiled=True)
    columns = activations
    image_data = lax.psum_scatter(
        lax.dot_general(
            columns, scaled, (((0,), (0,)), ((), ())), preferred_element_type=jnp.float32
        ).astype(jnp.bfloat16),
        "dp",
        scatter_dimension=0,
        tiled=True,
    ).astype(jnp.float32)
    new_image = image_data + prior_precision[0] * vector_now
    beta_old = beta_before[0]
    alpha_value = lax.psum(jnp.sum(new_image * vector_now), ("flat", "dp")) / total_cells
    residual = new_image - alpha_value * vector_now - beta_old * vector_before
    square = lax.psum(jnp.sum(residual * residual), ("flat", "dp")) / total_cells
    beta_value = jnp.sqrt(square + 1e-06)
    vector_next = residual / beta_value
    hadamard = hadamard_table()
    signed = (2 * sign_bits - 1).astype(jnp.float32) * vector_next
    rows_here = local_rows * out_width // (BLOCK * BLOCK)
    section_one = jnp.dot(signed.reshape(-1, BLOCK), hadamard, precision=lax.Precision.HIGHEST)
    section_one = section_one.reshape(rows_here, BLOCK * BLOCK)
    own_index = lax.axis_index(("flat", "dp"))
    column_block = lax.all_to_all(
        section_one.astype(jnp.bfloat16), ("flat", "dp"), split_axis=1, concat_axis=0, tiled=True
    ).astype(section_one.dtype)
    local_values = pick_dense(column_block, hadamard, own_index, kept_rows, kept_cols)
    sketch = lax.psum(local_values, ("flat", "dp"))
    return (vector_next, alpha_value.reshape(1), beta_value.reshape(1), sketch)


def solution(mesh):
    placed = (
        P(("groups", "dp"), "flat"),
        P(("groups", "dp")),
        P(("groups", "flat", "dp"), None),
        P(("groups", "flat", "dp"), None),
        P(("groups", "flat", "dp"), None),
        P("groups"),
        P("groups"),
        P("groups"),
        P("groups"),
    )
    return jax.shard_map(
        on_device,
        mesh=mesh,
        in_specs=placed,
        out_specs=(P(("groups", "flat", "dp"), None), P("groups"), P("groups"), P("groups")),
        check_vma=False,
    )
```

profile of v0, /device:TPU:0, one launch (start us, length us, event | category | flops | bytes accessed | tf_op | source)
XLA Modules:
  0.0 1159.3 jit_solution(15920801584408900253)
XLA Ops:
  7.2 0.0 all-gather.3.cloned.1.call-start
  7.2 9.4 convert_element_type.37
  16.6 0.0 all-gather.3.cloned.1.call-update
  16.6 0.0 copy-start.2
  16.6 0.0 reduce-scatter.5.cloned.1.call-start
  16.7 180.8 %all-gather.3.cloned.1.call-done = bf16[3584,4096]{1,0:T(8,128)(2,1)} async-done(((bf16[896,4096]{1,0:T(8,128)(2,1)}), bf16[3584,4096]{1,0:T(8,128)(2,1)}) %all-gather.3.cloned.1.call-update) | async-done | bytes 29360144 | tf_op jit(solution)/shard_map/all_gather | solution.py:61
  197.4 23.0 %convolution_convert_fusion.2 = bf16[512,4096]{1,0:T(8,128)(2,1)} fusion(bf16[512,3584]{1,0:T(8,128)(2,1)} %param.9, bf16[3584,4096]{1,0:T(8,128)(2,1)} %all-gather.3.cloned.1.call-done), kind=kOutput, calls=%fused_computation.10 | convolution fusion | flops 15034482688 | bytes 37224448 | tf_op jit(solution)/shard_map/dot_general | solution.py:59
  220.5 0.0 reduce-scatter.5.cloned.1.call-update
  220.5 0.0 all-gather.5.cloned.1.call-start
  220.5 76.9 %reduce-scatter.5.cloned.1.call-done = bf16[512,1024]{1,0:T(8,128)(2,1)} async-done(((bf16[512,4096]{1,0:T(8,128)(2,1)}), bf16[512,1024]{1,0:T(8,128)(2,1)}) %reduce-scatter.5.cloned.1.call-update) | async-done | bytes 1048592 | tf_op jit(solution)/shard_map/reduce_scatter | solution.py:64
  297.4 0.0 copy-done.2
  297.4 2.5 multiply_convert_fusion
  299.9 0.0 all-gather.5.cloned.1.call-update
  299.9 0.2 reduce-scatter.7.cloned.1.call-start
  300.2 81.2 %all-gather.5.cloned.1.call-done = bf16[512,4096]{1,0:T(8,128)(2,1)} async-done(((bf16[512,1024]{1,0:T(8,128)(2,1)}), bf16[512,4096]{1,0:T(8,128)(2,1)}) %all-gather.5.cloned.1.call-update) | async-done | bytes 4194320 | tf_op jit(solution)/shard_map/all_gather | solution.py:68
  381.4 22.3 %fusion = bf16[3584,4096]{0,1:T(8,128)(2,1)} fusion(bf16[512,4096]{1,0:T(8,128)(2,1)} %all-gather.5.cloned.1.call-done, bf16[512,3584]{1,0:T(8,128)(2,1)} %param.9), kind=kOutput, calls=%fused_computation.3 | convolution fusion | flops 15047065600 | bytes 37224448 | tf_op jit(solution)/shard_map/dot_general | solution.py:71
  403.7 37.0 %copy.36 = bf16[3584,4096]{1,0:T(8,128)(2,1)} copy(bf16[3584,4096]{0,1:T(8,128)(2,1)} %fusion) | data formatting | bytes 58720256
  440.7 0.0 reduce-scatter.7.cloned.1.call-update
  440.7 16.7 %copy.28 = f32[896,4096]{0,1:T(8,128)} copy(f32[896,4096]{1,0:T(8,128)} %param.11) | data formatting | bytes 29360128 | tf_op args[2]
  458.1 18.0 %copy.31 = f32[896,4096]{0,1:T(8,128)} copy(f32[896,4096]{1,0:T(8,128)} %param.12) | data formatting | bytes 29360128 | tf_op args[3]
  476.1 171.1 %reduce-scatter.7.cloned.1.call-done = bf16[896,4096]{1,0:T(8,128)(2,1)} async-done(((bf16[3584,4096]{1,0:T(8,128)(2,1)}), bf16[896,4096]{1,0:T(8,128)(2,1)}) %reduce-scatter.7.cloned.1.call-update) | async-done | bytes 7340048
  647.2 10.8 copy.37
  658.1 11.6 %multiply_reduce_fusion.1 = f32[]{:T(128)} fusion(f32[896,4096]{0,1:T(8,128)} %copy.28, bf16[896,4096]{0,1:T(8,128)(2,1)} %copy.37, f32[]{:T(128)} %bitcast.22), kind=kLoop, calls=%fused_computation.7 | loop fusion | flops 18350080 | bytes 22020104 | tf_op jit(solution)/shard_map/reduce_sum | solution.py:80
  670.4 32.9 %psum.21 = f32[]{:T(128)} all-reduce(f32[]{:T(128)} %multiply_reduce_fusion.1), channel_id=1, replica_groups=mesh['groups'=2,'flat'=4,'dp'=4] {'flat','dp'}, use_global_device_ids=true, to_apply=%region_3.0 | all-reduce | flops 1 | bytes 8 | tf_op jit(solution)/shard_map/psum | solution.py:80
  703.9 13.4 %multiply_reduce_fusion = f32[]{:T(128)} fusion(f32[896,4096]{0,1:T(8,128)} %copy.31, f32[]{:T(128)} %bitcast.25, f32[896,4096]{0,1:T(8,128)} %copy.28, f32[]{:T(128)} %div.28, f32[]{:T(128)} %bitcast.23, bf16[896,4096]{0,1:T(8,128)(2,1)} %copy.37), kind=kLoop, calls=%fused_computation.5 | loop fusion | flops 33030144 | bytes 36700176 | tf_op jit(solution)/shard_map/reduce_sum | solution.py:82
  717.3 16.1 %copy.32 = s32[896,4096]{0,1:T(8,128)} copy(s32[896,4096]{1,0:T(8,128)} %param.13) | data formatting | bytes 29360128 | tf_op args[4]
  733.4 30.3 %psum.22 = f32[]{:T(128)} all-reduce(f32[]{:T(128)} %multiply_reduce_fusion), channel_id=1, replica_groups=mesh['groups'=2,'flat'=4,'dp'=4] {'flat','dp'}, use_global_device_ids=true, to_apply=%region_5.0 | all-reduce | flops 1 | bytes 8 | tf_op jit(solution)/shard_map/psum | solution.py:82
  764.4 28.3 %convert_multiply_fusion = (f32[896,4096]{0,1:T(8,128)}, f32[896,4096]{0,1:T(8,128)}) fusion(s32[896,4096]{0,1:T(8,128)} %copy.32, f32[]{:T(128)} %sqrt.3, f32[896,4096]{0,1:T(8,128)} %copy.31, f32[]{:T(128)} %bitcast.26, f32[896,4096]{0,1:T(8,128)} %copy.28, f32[]{:T(128)} %div.28, f32[]{:T(128)} %bitcast.24, bf16[896,4096]{0,1:T(8,128)(2,1)} %copy.37), kind=kLoop, calls=%fused_computation.4 | loop fusion | flops 44040192 | bytes 80740368 | tf_op jit(solution)/shard_map/mul | solution.py:86
  792.7 16.1 %copy.33 = f32[896,4096]{1,0:T(8,128)} copy(f32[896,4096]{0,1:T(8,128)} %get-tuple-element.16) | data formatting | bytes 29360128 | tf_op jit(solution)/shard_map/mul | solution.py:86
  808.8 15.8 %reshape.33 = f32[28672,128]{1,0:T(8,128)} reshape(f32[896,4096]{1,0:T(8,128)} %copy.33) | data formatting | bytes 29360128 | tf_op jit(solution)/shard_map/reshape | solution.py:88
  824.6 15.6 %convolution_convert_fusion = bf16[28672,128]{1,0:T(8,128)(2,1)} fusion(f32[28672,128]{1,0:T(8,128)} %reshape.33), kind=kOutput, calls=%fused_computation.1 | convolution fusion | flops 5641240576 | bytes 22020096 | tf_op jit(solution)/shard_map/dot_general | solution.py:88
  840.3 11.8 %convert_element_type.47 = bf16[224,16,1024]{2,1,0:T(8,128)(2,1)} reshape(bf16[28672,128]{1,0:T(8,128)(2,1)} %convolution_convert_fusion) | data formatting | bytes 14680064 | tf_op jit(solution)/shard_map/convert_element_type | solution.py:92
  852.0 0.0 copy-start
  852.0 0.0 copy-start.1
  852.0 10.2 copy.34
  862.2 5.0 all-to-all-start
  867.2 0.0 copy-done
  867.2 0.0 copy-done.1
  867.2 16.1 %copy.35 = f32[896,4096]{1,0:T(8,128)} copy(f32[896,4096]{0,1:T(8,128)} %get-tuple-element.17) | data formatting | bytes 29360128
  883.3 116.0 %all-to-all-done = bf16[224,16,1024]{2,0,1:T(8,128)(2,1)} async-done(((bf16[224,16,1024]{2,0,1:T(8,128)(2,1)}), bf16[224,16,1024]{2,0,1:T(8,128)(2,1)}, u32[]{:S(2)}, u32[]{:S(2)}) %all-to-all-start) | async-done | bytes 7340064 | tf_op jit(solution)/shard_map/all_to_all | solution.py:91
  999.3 12.7 %fusion.1 = f32[28,1024,128]{1,2,0:T(8,128)} fusion(bf16[28,128,1024]{2,1,0:T(8,128)(2,1)} %bitcast.6), kind=kOutput, calls=%fused_computation.12 | convolution fusion | flops 5637570560 | bytes 22020096 | tf_op jit(solution)/shard_map/ri,bic->brc/dot_general | solution.py:26
  1012.0 50.1 %gather_fusion = f32[4096]{0:T(1024)S(1)} fusion(f32[3584,1024]{1,0:T(8,128)} %bitcast.27, s32[4096]{0:T(1024)S(1)} %fusion.5), kind=kCustom, calls=%fused_computation | custom fusion | bytes 65536 | tf_op jit(solution)/shard_map/gather | solution.py:36
  1062.1 88.3 %psum.23 = f32[4096]{0:T(1024)} all-reduce(f32[4096]{0:T(1024)S(1)} %and_select_fusion), channel_id=1, replica_groups=mesh['groups'=2,'flat'=4,'dp'=4] {'flat','dp'}, use_global_device_ids=true, to_apply=%region_6.7 | all-reduce | flops 4096 | bytes 32768 | tf_op jit(solution)/shard_map/psum | solution.py:95
  (2 shorter events, 0.0 us)
Async XLA Ops:
  7.2 190.3 %all-gather.3.cloned.1.call-start = ((), (), s32[]{:S(2)}) async-start(), calls=%async_computation.3 | async-start | bytes 36700160 | tf_op jit(solution)/shard_map/all_gather | solution.py:61
  16.6 280.8 %copy-start.2 = (f32[512]{0:T(512)S(1)}, f32[512]{0:T(512)}, u32[]{:S(2)}) copy-start(f32[512]{0:T(512)} %param.10) | copy-start | bytes 6148
  16.6 280.8 %reduce-scatter.5.cloned.1.call-start = ((), (), s32[]{:S(2)}) async-start(), calls=%async_computation.4 | async-start | bytes 5242880 | tf_op jit(solution)/shard_map/reduce_scatter | solution.py:64
  220.5 160.9 %all-gather.5.cloned.1.call-start = ((), (), s32[]{:S(2)}) async-start(), calls=%async_computation.5 | async-start | bytes 5242880 | tf_op jit(solution)/shard_map/all_gather | solution.py:68
  299.9 347.3 %reduce-scatter.7.cloned.1.call-start = ((), (), s32[]{:S(2)}) async-start(), calls=%async_computation.6 | async-start | bytes 36700160
  852.0 15.2 %copy-start = (s32[4096]{0:T(1024)S(1)}, s32[4096]{0:T(1024)}, u32[]{:S(2)}) copy-start(s32[4096]{0:T(1024)} %param.17) | copy-start | bytes 49156
  852.0 15.2 %copy-start.1 = (s32[4096]{0:T(1024)S(1)}, s32[4096]{0:T(1024)}, u32[]{:S(2)}) copy-start(s32[4096]{0:T(1024)} %param.16) | copy-start | bytes 49156
  862.2 137.1 %all-to-all-start = ((bf16[224,16,1024]{2,0,1:T(8,128)(2,1)}), bf16[224,16,1024]{2,0,1:T(8,128)(2,1)}, u32[]{:S(2)}, u32[]{:S(2)}) async-start(bf16[224,16,1024]{2,0,1:T(8,128)(2,1)} %copy.34), calls=%async_computation.1 | async-start | bytes 14680064 | tf_op jit(solution)/shard_map/all_to_all | solution.py:91
Sparse Core Ops, SparseCore 0:
  16.7 180.6 all-gather.2
  220.6 76.7 reduce-scatter.4
  300.1 81.2 all-gather.4
  440.8 206.3 reduce-scatter.6
where the time goes:
time: 1160 us
  waiting for transfers between devices  626 us (54%)
  local copies, waits for them, and re-layouts  219 us (19%)
  blocking collectives  152 us (13%)
  matrix products  73.6 us (6%)
  other arithmetic  65.2 us (6%)
  between operations  18.8 us (2%)
    all_gather x1, waiting for transfers between devices, on_device(): lax.all_gather(vector_half, 'dp', axis=0, tiled=True)  181 us
    unnamed x5, waiting for transfers between devices  171 us
    all_to_all x1, waiting for transfers between devices, on_device(): lax.all_to_all(section_one.astype(jnp.bfloat16), ('flat', 'dp'), split_ax...  116 us
    unnamed x12, local copies, waits for them, and re-layouts  115 us
    psum x1, blocking collectives, on_device(): sketch = lax.psum(local_values, ('flat', 'dp'))  88.3 us
    all_gather x1, waiting for transfers between devices, on_device(): scaled = lax.all_gather(scaled_share, 'flat', axis=1, tiled=True)  81.2 us
    reduce_scatter x1, waiting for transfers between devices, on_device(): lax.psum_scatter(partial_out.astype(jnp.bfloat16), 'flat', scatter_dimens...  76.9 us
    gather x1, local copies, waits for them, and re-layouts, pick_dense(): return jnp.where(inside, section_two[kept_rows, local_col], 0.0)  50.1 us
  transfers between devices with their start and end apart: 5, of which 5 were waited for; matrix products, arithmetic and copies ran while one was open for 4% of the time, Pallas kernels for 0%

commit v1 on v0

--- a/solution.py
+++ b/solution.py
@@ -92,7 +92,7 @@
         section_one.astype(jnp.bfloat16), ("flat", "dp"), split_axis=1, concat_axis=0, tiled=True
     ).astype(section_one.dtype)
     local_values = pick_dense(column_block, hadamard, own_index, kept_rows, kept_cols)
-    sketch = lax.psum(local_values, ("flat", "dp"))
+    sketch = jnp.sum(lax.all_gather(local_values, ("flat", "dp")), axis=0)
     return (vector_next, alpha_value.reshape(1), beta_value.reshape(1), sketch)
 
 

time: 1160 us -> 1130 us (0.974)
  blocking collectives: 152 us -> 112 us
    psum x1 -> x0, blocking collectives: 88.3 us -> none  [on_device(): sketch = lax.psum(local_values, ('flat', 'dp'))]
    all_gather x0 -> x1, blocking collectives: none -> 48.9 us  [on_device(): sketch = jnp.sum(lax.all_gather(local_values, ('flat', 'dp')), axis=0)]
  transfers between devices with their start and end apart: 5 -> 5, of which waited for: 5 -> 5; matrix products, arithmetic and copies ran while one was open for 4% -> 5% of each run, Pallas kernels for 0% -> 0%
where the time goes in v1:
time: 1130 us; the launch traced here: 1120 us
  waiting for transfers between devices  626 us (55%)
  local copies, waits for them, and re-layouts  219 us (19%)
  blocking collectives  112 us (10%)
  matrix products  73.6 us (7%)
  other arithmetic  65.8 us (6%)
  between operations  18.8 us (2%)
    all_gather x1, waiting for transfers between devices, on_device(): lax.all_gather(vector_half, 'dp', axis=0, tiled=True)  181 us
    unnamed x5, waiting for transfers between devices  171 us
    all_to_all x1, waiting for transfers between devices, on_device(): lax.all_to_all(section_one.astype(jnp.bfloat16), ('flat', 'dp'), split_ax...  116 us
    unnamed x12, local copies, waits for them, and re-layouts  115 us
    all_gather x1, waiting for transfers between devices, on_device(): scaled = lax.all_gather(scaled_share, 'flat', axis=1, tiled=True)  81.2 us
    reduce_scatter x1, waiting for transfers between devices, on_device(): lax.psum_scatter(partial_out.astype(jnp.bfloat16), 'flat', scatter_dimens...  76.9 us
    gather x1, local copies, waits for them, and re-layouts, pick_dense(): return jnp.where(inside, section_two[kept_rows, local_col], 0.0)  50.1 us
    all_gather x1, blocking collectives, on_device(): sketch = jnp.sum(lax.all_gather(local_values, ('flat', 'dp')), axis=0)  48.9 us
  transfers between devices with their start and end apart: 5, of which 5 were waited for; matrix products, arithmetic and copies ran while one was open for 5% of the time, Pallas kernels for 0%

profile of v1, /device:TPU:0, one launch (start us, length us, event | category | flops | bytes accessed | tf_op | source)
XLA Modules:
  0.0 1120.5 jit_solution(626506620005076519)
XLA Ops:
  7.2 0.0 all-gather.4.cloned.1.call-start
  7.2 9.4 convert_element_type.37
  16.6 0.0 all-gather.4.cloned.1.call-update
  16.6 0.0 copy-start.2
  16.6 0.0 reduce-scatter.5.cloned.1.call-start
  16.7 180.8 %all-gather.4.cloned.1.call-done = bf16[3584,4096]{1,0:T(8,128)(2,1)} async-done(((bf16[896,4096]{1,0:T(8,128)(2,1)}), bf16[3584,4096]{1,0:T(8,128)(2,1)}) %all-gather.4.cloned.1.call-update) | async-done | bytes 29360144 | tf_op jit(solution)/shard_map/all_gather | solution.py:61
  197.4 23.0 %convolution_convert_fusion.2 = bf16[512,4096]{1,0:T(8,128)(2,1)} fusion(bf16[512,3584]{1,0:T(8,128)(2,1)} %param.9, bf16[3584,4096]{1,0:T(8,128)(2,1)} %all-gather.4.cloned.1.call-done), kind=kOutput, calls=%fused_computation.10 | convolution fusion | flops 15034482688 | bytes 37224448 | tf_op jit(solution)/shard_map/dot_general | solution.py:59
  220.5 0.0 reduce-scatter.5.cloned.1.call-update
  220.5 0.0 all-gather.6.cloned.1.call-start
  220.5 76.9 %reduce-scatter.5.cloned.1.call-done = bf16[512,1024]{1,0:T(8,128)(2,1)} async-done(((bf16[512,4096]{1,0:T(8,128)(2,1)}), bf16[512,1024]{1,0:T(8,128)(2,1)}) %reduce-scatter.5.cloned.1.call-update) | async-done | bytes 1048592 | tf_op jit(solution)/shard_map/reduce_scatter | solution.py:64
  297.4 0.0 copy-done.2
  297.4 2.5 multiply_convert_fusion
  299.9 0.0 all-gather.6.cloned.1.call-update
  299.9 0.2 reduce-scatter.7.cloned.1.call-start
  300.2 81.2 %all-gather.6.cloned.1.call-done = bf16[512,4096]{1,0:T(8,128)(2,1)} async-done(((bf16[512,1024]{1,0:T(8,128)(2,1)}), bf16[512,4096]{1,0:T(8,128)(2,1)}) %all-gather.6.cloned.1.call-update) | async-done | bytes 4194320 | tf_op jit(solution)/shard_map/all_gather | solution.py:68
  381.4 22.3 %fusion = bf16[3584,4096]{0,1:T(8,128)(2,1)} fusion(bf16[512,4096]{1,0:T(8,128)(2,1)} %all-gather.6.cloned.1.call-done, bf16[512,3584]{1,0:T(8,128)(2,1)} %param.9), kind=kOutput, calls=%fused_computation.3 | convolution fusion | flops 15047065600 | bytes 37224448 | tf_op jit(solution)/shard_map/dot_general | solution.py:71
  403.7 37.0 %copy.44 = bf16[3584,4096]{1,0:T(8,128)(2,1)} copy(bf16[3584,4096]{0,1:T(8,128)(2,1)} %fusion) | data formatting | bytes 58720256
  440.7 0.0 reduce-scatter.7.cloned.1.call-update
  440.7 16.7 %copy.36 = f32[896,4096]{0,1:T(8,128)} copy(f32[896,4096]{1,0:T(8,128)} %param.11) | data formatting | bytes 29360128 | tf_op args[2]
  458.1 18.0 %copy.39 = f32[896,4096]{0,1:T(8,128)} copy(f32[896,4096]{1,0:T(8,128)} %param.12) | data formatting | bytes 29360128 | tf_op args[3]
  476.1 171.1 %reduce-scatter.7.cloned.1.call-done = bf16[896,4096]{1,0:T(8,128)(2,1)} async-done(((bf16[3584,4096]{1,0:T(8,128)(2,1)}), bf16[896,4096]{1,0:T(8,128)(2,1)}) %reduce-scatter.7.cloned.1.call-update) | async-done | bytes 7340048
  647.2 10.8 copy.45
  658.1 11.6 %multiply_reduce_fusion.1 = f32[]{:T(128)} fusion(f32[896,4096]{0,1:T(8,128)} %copy.36, bf16[896,4096]{0,1:T(8,128)(2,1)} %copy.45, f32[]{:T(128)} %bitcast.22), kind=kLoop, calls=%fused_computation.7 | loop fusion | flops 18350080 | bytes 22020104 | tf_op jit(solution)/shard_map/reduce_sum | solution.py:80
  670.4 32.9 %psum.14 = f32[]{:T(128)} all-reduce(f32[]{:T(128)} %multiply_reduce_fusion.1), channel_id=1, replica_groups=mesh['groups'=2,'flat'=4,'dp'=4] {'flat','dp'}, use_global_device_ids=true, to_apply=%region_3.0 | all-reduce | flops 1 | bytes 8 | tf_op jit(solution)/shard_map/psum | solution.py:80
  703.9 13.4 %multiply_reduce_fusion = f32[]{:T(128)} fusion(f32[896,4096]{0,1:T(8,128)} %copy.39, f32[]{:T(128)} %bitcast.25, f32[896,4096]{0,1:T(8,128)} %copy.36, f32[]{:T(128)} %div.28, f32[]{:T(128)} %bitcast.23, bf16[896,4096]{0,1:T(8,128)(2,1)} %copy.45), kind=kLoop, calls=%fused_computation.5 | loop fusion | flops 33030144 | bytes 36700176 | tf_op jit(solution)/shard_map/reduce_sum | solution.py:82
  717.3 16.1 %copy.40 = s32[896,4096]{0,1:T(8,128)} copy(s32[896,4096]{1,0:T(8,128)} %param.13) | data formatting | bytes 29360128 | tf_op args[4]
  733.4 30.3 %psum.15 = f32[]{:T(128)} all-reduce(f32[]{:T(128)} %multiply_reduce_fusion), channel_id=1, replica_groups=mesh['groups'=2,'flat'=4,'dp'=4] {'flat','dp'}, use_global_device_ids=true, to_apply=%region_5.0 | all-reduce | flops 1 | bytes 8 | tf_op jit(solution)/shard_map/psum | solution.py:82
  764.4 28.3 %convert_multiply_fusion = (f32[896,4096]{0,1:T(8,128)}, f32[896,4096]{0,1:T(8,128)}) fusion(s32[896,4096]{0,1:T(8,128)} %copy.40, f32[]{:T(128)} %sqrt.3, f32[896,4096]{0,1:T(8,128)} %copy.39, f32[]{:T(128)} %bitcast.26, f32[896,4096]{0,1:T(8,128)} %copy.36, f32[]{:T(128)} %div.28, f32[]{:T(128)} %bitcast.24, bf16[896,4096]{0,1:T(8,128)(2,1)} %copy.45), kind=kLoop, calls=%fused_computation.4 | loop fusion | flops 44040192 | bytes 80740368 | tf_op jit(solution)/shard_map/mul | solution.py:86
  792.7 16.1 %copy.41 = f32[896,4096]{1,0:T(8,128)} copy(f32[896,4096]{0,1:T(8,128)} %get-tuple-element.20) | data formatting | bytes 29360128 | tf_op jit(solution)/shard_map/mul | solution.py:86
  808.8 15.8 %reshape.33 = f32[28672,128]{1,0:T(8,128)} reshape(f32[896,4096]{1,0:T(8,128)} %copy.41) | data formatting | bytes 29360128 | tf_op jit(solution)/shard_map/reshape | solution.py:88
  824.6 15.6 %convolution_convert_fusion = bf16[28672,128]{1,0:T(8,128)(2,1)} fusion(f32[28672,128]{1,0:T(8,128)} %reshape.33), kind=kOutput, calls=%fused_computation.1 | convolution fusion | flops 5641240576 | bytes 22020096 | tf_op jit(solution)/shard_map/dot_general | solution.py:88
  840.3 11.8 %convert_element_type.47 = bf16[224,16,1024]{2,1,0:T(8,128)(2,1)} reshape(bf16[28672,128]{1,0:T(8,128)(2,1)} %convolution_convert_fusion) | data formatting | bytes 14680064 | tf_op jit(solution)/shard_map/convert_element_type | solution.py:92
  852.0 0.0 copy-start
  852.0 0.0 copy-start.1
  852.0 10.2 copy.42
  862.2 5.0 all-to-all-start
  867.2 0.0 copy-done
  867.2 0.0 copy-done.1
  867.2 16.1 %copy.43 = f32[896,4096]{1,0:T(8,128)} copy(f32[896,4096]{0,1:T(8,128)} %get-tuple-element.21) | data formatting | bytes 29360128
  883.3 116.0 %all-to-all-done = bf16[224,16,1024]{2,0,1:T(8,128)(2,1)} async-done(((bf16[224,16,1024]{2,0,1:T(8,128)(2,1)}), bf16[224,16,1024]{2,0,1:T(8,128)(2,1)}, u32[]{:S(2)}, u32[]{:S(2)}) %all-to-all-start) | async-done | bytes 7340064 | tf_op jit(solution)/shard_map/all_to_all | solution.py:91
  999.3 12.7 %fusion.1 = f32[28,1024,128]{1,2,0:T(8,128)} fusion(bf16[28,128,1024]{2,1,0:T(8,128)(2,1)} %bitcast.6), kind=kOutput, calls=%fused_computation.12 | convolution fusion | flops 5637570560 | bytes 22020096 | tf_op jit(solution)/shard_map/ri,bic->brc/dot_general | solution.py:26
  1012.0 50.1 %gather_fusion = f32[4096]{0:T(1024)S(1)} fusion(f32[3584,1024]{1,0:T(8,128)} %bitcast.27, s32[4096]{0:T(1024)S(1)} %fusion.5), kind=kCustom, calls=%fused_computation | custom fusion | bytes 65536 | tf_op jit(solution)/shard_map/gather | solution.py:36
  1062.1 48.9 %all-gather = f32[65536]{0:T(1024)S(1)} all-gather(f32[4096]{0:T(1024)S(1)} %and_select_fusion), channel_id=2, replica_groups=mesh['groups'=2,'flat'=4,'dp'=4] {'flat','dp'}, dimensions={0}, use_global_device_ids=true | all-gather | bytes 278528 | tf_op jit(solution)/shard_map/all_gather | solution.py:95
  1111.0 0.1 reshape.42
  1111.0 0.6 reduce_sum.29
  (2 shorter events, 0.0 us)
Async XLA Ops:
  7.2 190.3 %all-gather.4.cloned.1.call-start = ((), (), s32[]{:S(2)}) async-start(), calls=%async_computation.3 | async-start | bytes 36700160 | tf_op jit(solution)/shard_map/all_gather | solution.py:61
  16.6 280.8 %copy-start.2 = (f32[512]{0:T(512)S(1)}, f32[512]{0:T(512)}, u32[]{:S(2)}) copy-start(f32[512]{0:T(512)} %param.10) | copy-start | bytes 6148
  16.6 280.8 %reduce-scatter.5.cloned.1.call-start = ((), (), s32[]{:S(2)}) async-start(), calls=%async_computation.4 | async-start | bytes 5242880 | tf_op jit(solution)/shard_map/reduce_scatter | solution.py:64
  220.5 160.9 %all-gather.6.cloned.1.call-start = ((), (), s32[]{:S(2)}) async-start(), calls=%async_computation.5 | async-start | bytes 5242880 | tf_op jit(solution)/shard_map/all_gather | solution.py:68
  299.9 347.3 %reduce-scatter.7.cloned.1.call-start = ((), (), s32[]{:S(2)}) async-start(), calls=%async_computation.6 | async-start | bytes 36700160
  852.0 15.2 %copy-start = (s32[4096]{0:T(1024)S(1)}, s32[4096]{0:T(1024)}, u32[]{:S(2)}) copy-start(s32[4096]{0:T(1024)} %param.17) | copy-start | bytes 49156
  852.0 15.2 %copy-start.1 = (s32[4096]{0:T(1024)S(1)}, s32[4096]{0:T(1024)}, u32[]{:S(2)}) copy-start(s32[4096]{0:T(1024)} %param.16) | copy-start | bytes 49156
  862.2 137.1 %all-to-all-start = ((bf16[224,16,1024]{2,0,1:T(8,128)(2,1)}), bf16[224,16,1024]{2,0,1:T(8,128)(2,1)}, u32[]{:S(2)}, u32[]{:S(2)}) async-start(bf16[224,16,1024]{2,0,1:T(8,128)(2,1)} %copy.42), calls=%async_computation.1 | async-start | bytes 14680064 | tf_op jit(solution)/shard_map/all_to_all | solution.py:91
Sparse Core Ops, SparseCore 0:
  16.7 180.6 all-gather.3
  220.6 76.7 reduce-scatter.4
  300.1 81.2 all-gather.5
  440.8 206.3 reduce-scatter.6
